TPU v7x, 32 devices: a whole 2x2x4 slice. The times are simulated.
32 devices in a mesh: row: 2 (over x), col: 16 (over z, y, core).
Axes of the slice: x: 2, y: 2, z: 4, core: 2. Of those that a mesh axis runs over, the one named last changes fastest.
Arguments:
- tokens: bfloat16 [128, 7168], P(('row', 'col')), may hold values from -6 to 6
- gate_up: bfloat16 [16, 2, 1536, 7168], P('col', None, 'row'), may hold values from -0.0625 to 0.0625
- down: bfloat16 [16, 1536, 7168], P('col', None, 'row'), may hold values from -0.15625 to 0.15625
- expert_ids: int32 [128, 8], replicated, may hold values from 0 to 15, all different within a row; in each aligned block of 64 rows (0 to 63, 64 to 127, ...) at most 48 rows name the same one
- gate_weights: float32 [128, 8], replicated, may hold values from 0.05 to 1
- capacity: int32 [16], replicated, may hold values from 24 to 48
Outputs:
- routed_out: bfloat16 [128, 7168], P(('row', 'col'))
Inputs may be any that keep to these rules, and one draw needn't show every extreme that they name: `expert_ids`: each row names 8 different experts; within each aligned group of 64 rows no expert is named by more than 48 rows.
All inputs are finite; a program needn't handle non-finite values.
Results may differ from a plain program's by a relative error of at most 0.0063.
Values may be sent and summed in bfloat16 or wider, within the bound.
A program may use at most 64 MiB of HBM per device.

v0:
```python
import jax
import jax.numpy as jnp
from jax import lax
from jax.sharding import PartitionSpec as P

TOP = 8


def expert_slots(expert_ids, gate_weights, capacity, expert, block_rows, slot_cap):
    total_rows = expert_ids.shape[0]
    member = expert_ids == expert
    hit_count = jnp.sum(member.astype(jnp.int32), axis=1)
    grouped = hit_count.reshape(total_rows // block_rows, block_rows)
    rank_in = (jnp.cumsum(grouped, axis=1) - grouped).reshape(total_rows)
    cap_here = lax.dynamic_index_in_dim(capacity, expert, 0, keepdims=False)
    usable = (hit_count > 0) & (rank_in < cap_here)
    weights = jnp.sum(jnp.where(member, gate_weights, 0.0), axis=1)
    groups = jnp.arange(total_rows, dtype=jnp.int32) // block_rows
    slot_ids = jnp.where(usable, groups * slot_cap + rank_in, -1)
    return (slot_ids, weights)


def local(tokens, gate_up, down, expert_ids, gate_weights, capacity):
    col_count = lax.axis_size("col")
    row_count = lax.axis_size("row")
    col_index = lax.axis_index("col")
    row_index = lax.axis_index("row")
    tok_dev = tokens.shape[0]
    block_rows = col_count * tok_dev
    slot_cap = min(3 * tok_dev * TOP // 2, block_rows)
    slot_count = row_count * slot_cap
    total_rows = expert_ids.shape[0]
    slot_ids, weights = expert_slots(
        expert_ids, gate_weights, capacity, col_index, block_rows, slot_cap
    )
    group_tokens = lax.all_gather(tokens, "col", axis=0, tiled=True)
    local_slots = (
        lax.dynamic_slice_in_dim(slot_ids, row_index * block_rows, block_rows)
        - row_index * slot_cap
    )
    cap_index = jnp.arange(slot_cap, dtype=jnp.int32)
    select = (cap_index[:, None] == local_slots[None, :]).astype(jnp.bfloat16)
    picked = jnp.dot(select, group_tokens, preferred_element_type=jnp.float32).astype(jnp.bfloat16)
    w_gate = gate_up[0, 0]
    w_up = gate_up[0, 1]
    contract = (((1,), (1,)), ((), ()))
    piece = lax.all_gather(picked, "row", axis=0, tiled=True)
    gate_part = lax.dot_general(piece, w_gate, contract, preferred_element_type=jnp.float32)
    up_part = lax.dot_general(piece, w_up, contract, preferred_element_type=jnp.float32)
    hidden = (jax.nn.silu(gate_part) * up_part).astype(jnp.bfloat16)
    w_down = down[0]
    outputs = jnp.dot(
        lax.all_gather(hidden, "row", axis=1, tiled=True),
        w_down,
        preferred_element_type=jnp.float32,
    ).astype(jnp.bfloat16)

    def by_column(values):
        return values.reshape(row_count, col_count, tok_dev).transpose(1, 0, 2).reshape(total_rows)

    column_slots = by_column(slot_ids)
    column_weights = by_column(weights)
    slot_index = jnp.arange(slot_count, dtype=jnp.int32)
    combine = jnp.where(
        column_slots[:, None] == slot_index[None, :], column_weights[:, None], 0.0
    ).astype(jnp.bfloat16)
    summed = lax.psum_scatter(
        jnp.dot(combine, outputs, preferred_element_type=jnp.float32),
        "col",
        scatter_dimension=0,
        tiled=True,
    )
    own_rows = lax.all_to_all(
        summed.astype(jnp.bfloat16), "row", split_axis=0, concat_axis=1, tiled=True
    ).astype(summed.dtype)
    return own_rows.astype(jnp.bfloat16)


def solution(mesh):
    in_specs = (
        P(("row", "col"), None),
        P("col", None, "row", None),
        P("col", None, "row"),
        P(),
        P(),
        P(),
    )
    out_specs = P(("row", "col"), None)
    return jax.shard_map(local, mesh=mesh, in_specs=in_specs, out_specs=out_specs, check_vma=False)
```

profile of v0, /device:TPU:0, one launch (start us, length us, event | category | flops | bytes accessed | tf_op | source)
XLA Modules:
  0.0 164.7 jit_solution(8550963724826204604)
XLA Ops:
  6.5 0.7 select_reduce_fusion
  7.3 0.1 reshape.24
  7.4 0.2 reduce_window_sum.15
  7.6 0.1 reduce_window_sum.17
  7.7 26.1 %all-gather = bf16[16,4,7168]{2,1,0:T(4,128)(2,1)S(1)} all-gather(bf16[1,4,7168]{2,1,0:T(4,128)(2,1)} %bitcast.30), channel_id=1, replica_groups=mesh['row'=2,'col'=16] {'col'}, dimensions={0}, use_global_device_ids=true | all-gather | bytes 974848 | tf_op jit(solution)/shard_map/all_gather | solution.py:36
  33.8 0.2 reshape.27
  34.0 1.2 dynamic_slice.7
  35.2 0.7 and_select_fusion.1
  35.9 0.1 dynamic-slice_subtract_fusion
  36.0 1.2 convolution_convert_fusion
  37.4 0.1 reduce_sum.21
  37.5 0.1 reshape.25
  37.6 0.1 broadcast_in_dim.24
  37.7 0.7 fusion.27
  38.4 0.1 eq.36
  38.5 21.1 %all-gather.3.cloned.1.call-done = bf16[96,7168]{1,0:T(8,128)(2,1)} async-done(((bf16[48,7168]{1,0:T(8,128)(2,1)}), bf16[96,7168]{1,0:T(8,128)(2,1)}) %all-gather.3.cloned.1.call-update) | async-done | bytes 1376272 | tf_op jit(solution)/shard_map/all_gather | solution.py:47
  59.7 7.8 %fusion.4 = f32[96,768]{1,0:T(8,128)S(1)} fusion(bf16[96,7168]{1,0:T(8,128)(2,1)} %all-gather.3.cloned.1.call-done, bf16[1,2,768,7168]{3,2,1,0:T(8,128)(2,1)} %param.7), kind=kOutput, calls=%fused_computation.4 | convolution fusion | flops 1056964608 | bytes 12681216 | tf_op jit(solution)/shard_map/dot_general | solution.py:48
  67.5 7.7 %fusion.17 = bf16[96,768]{1,0:T(8,128)(2,1)S(1)} fusion(bf16[96,7168]{1,0:T(8,128)(2,1)S(1)} %copy-done, bf16[1,2,768,7168]{3,2,1,0:T(8,128)(2,1)} %param.7, f32[96,768]{1,0:T(8,128)S(1)} %fusion.4), kind=kOutput, calls=%fused_computation.12 | convolution fusion | flops 1057406976 | bytes 12828672 | tf_op jit(solution)/shard_map/dot_general | solution.py:49
  75.2 6.3 %all_gather.11 = bf16[96,1536]{1,0:T(8,128)(2,1)S(1)} all-gather(bf16[96,768]{1,0:T(8,128)(2,1)S(1)} %fusion.17), channel_id=1, replica_groups=mesh['row'=2,'col'=16] {'row'}, dimensions={1}, use_global_device_ids=true | all-gather | bytes 442368 | tf_op jit(solution)/shard_map/all_gather | solution.py:53
  81.5 7.5 %fusion.12 = f32[128,3584]{1,0:T(8,128)} fusion(bf16[96,1536]{1,0:T(8,128)(2,1)S(1)} %all_gather.11, bf16[1,1536,3584]{2,1,0:T(8,128)(2,1)} %param.8, bf16[128]{0:T(256)(128)(2,1)S(1)} %broadcast_in_dim.24, s32[128]{0:T(128)S(1)} %eq.36), kind=kOutput, calls=%fused_computation.10 | convolution fusion | flops 1145413632 | bytes 13140736 | tf_op jit(solution)/shard_map/dot_general | solution.py:68
  89.0 60.7 %reduce-scatter.2.cloned.1.call-done = f32[8,3584]{1,0:T(8,128)} async-done(((f32[128,3584]{1,0:T(8,128)}), f32[8,3584]{1,0:T(8,128)}) %reduce-scatter.2.cloned.1.call-update) | async-done | bytes 114704 | tf_op jit(solution)/shard_map/reduce_scatter | solution.py:67
  149.7 0.9 convert_element_type.26
  150.6 6.6 %all_to_all.19 = bf16[2,4,3584]{2,1,0:T(4,128)(2,1)S(1)} all-to-all(bf16[2,4,3584]{2,1,0:T(4,128)(2,1)S(1)} %all_to_all.14), channel_id=1, replica_groups=mesh['row'=2,'col'=16] {'row'}, dimensions={0} | all-to-all | bytes 114688 | tf_op jit(solution)/shard_map/all_to_all | solution.py:73
  157.2 0.6 copy.17
  (11 shorter events, 0.2 us)
Async XLA Ops:
  6.5 53.1 %all-gather.3.cloned.1.call-start = ((), (), s32[]{:S(2)}) async-start(), calls=%async_computation.2 | async-start | bytes 2064384 | tf_op jit(solution)/shard_map/all_gather | solution.py:47
  37.2 112.5 %reduce-scatter.2.cloned.1.call-start = ((), (), s32[]{:S(2)}) async-start(), calls=%async_computation.3 | async-start | bytes 1949696 | tf_op jit(solution)/shard_map/reduce_scatter | solution.py:67
  59.7 7.9 %copy-start = (bf16[96,7168]{1,0:T(8,128)(2,1)S(1)}, bf16[96,7168]{1,0:T(8,128)(2,1)}, u32[]{:S(2)}) copy-start(bf16[96,7168]{1,0:T(8,128)(2,1)} %all-gather.3.cloned.1.call-done) | copy-start | bytes 4128772
Sparse Core Ops, SparseCore 0:
  37.3 22.2 all-gather.2
  89.1 60.5 reduce-scatter.1
where the time goes:
time: 165 us
  waiting for transfers between devices  81.8 us (50%)
  blocking collectives  39 us (24%)
  matrix products  24.2 us (15%)
  between operations  13.5 us (8%)
  other arithmetic  3.29 us (2%)
  local copies, waits for them, and re-layouts  2.8 us (2%)
    reduce_scatter x1, waiting for transfers between devices, local(): lax.psum_scatter(jnp.dot(combine, outputs, preferred_element_type=jnp.flo...  60.7 us
    all_gather x1, blocking collectives, local(): group_tokens = lax.all_gather(tokens, 'col', axis=0, tiled=True)  26.1 us
    all_gather x1, waiting for transfers between devices, local(): piece = lax.all_gather(picked, 'row', axis=0, tiled=True)  21.1 us
    dot_general x1, matrix products, local(): lax.dot_general(piece, w_gate, contract, preferred_element_type=jnp.float32)  7.85 us
    dot_general x1, matrix products, local(): lax.dot_general(piece, w_up, contract, preferred_element_type=jnp.float32)  7.68 us
    dot_general x1, matrix products, local(): jnp.dot(combine, outputs, preferred_element_type=jnp.float32)  7.5 us
    all_to_all x1, blocking collectives, local(): lax.all_to_all(summed.astype(jnp.bfloat16), 'row', split_axis=0, concat_a...  6.6 us
    all_gather x1, blocking collectives, local(): lax.all_gather(hidden, 'row', axis=1, tiled=True)  6.27 us
  transfers between devices with their start and end apart: 2, of which 2 were waited for; matrix products, arithmetic and copies ran while one was open for 1% of the time, Pallas kernels for 0%

commit v1 on v0

--- a/solution.py
+++ b/solution.py
@@ -1,9 +1,345 @@
+import functools
+
 import jax
 import jax.numpy as jnp
 from jax import lax
+from jax.experimental import pallas as pl
+from jax.experimental.pallas import tpu as pltpu
 from jax.sharding import PartitionSpec as P
 
 TOP = 8
+MESH = pl.DeviceIdType.MESH
+CORES, YS, ZS, ROWS = 2, 2, 4, 2
+TILE = 256
+
+
+def fused_kernel(
+    nk,
+    nr,
+    tokens_ref,
+    ids_ref,
+    weights_ref,
+    capacity_ref,
+    gate_up_ref,
+    down_ref,
+    out_ref,
+    wgu,
+    wd,
+    xbuf,
+    x2d,
+    acc,
+    hid,
+    yacc,
+    zf,
+    r1_out,
+    r1_in,
+    p1,
+    r2_out,
+    r2_in,
+    p2,
+    r3_out,
+    r3_in,
+    p3,
+    r4_in,
+    load_sem,
+    g_send,
+    g_recv,
+    h_send,
+    h_recv,
+    r_send,
+    r_recv,
+):
+    row = lax.axis_index("row")
+    col = lax.axis_index("col")
+    core = col % CORES
+    y = (col // CORES) % YS
+    z = col // (CORES * YS)
+    tok_dev, width = tokens_ref.shape
+    kc = width // nk
+    tokens = x2d.shape[1]
+    half = down_ref.shape[2]
+    nc = half // nr
+    hidden = gate_up_ref.shape[2]
+    tiles = hidden // TILE
+
+    x_peer = (1 - row, col)
+    y_peer = (row, z * 4 + (1 - y) * 2 + core)
+    core_peer = (row, z * 4 + y * 2 + 1 - core)
+    z_places = (z + 1 - 2 * (z % 2), (z + 2) % ZS, ZS - 1 - z)
+    z_peers = [(row, place * 4 + y * 2 + core) for place in z_places]
+
+    def load_gu(k):
+        columns = pl.ds(k * kc, kc)
+        return pltpu.make_async_copy(
+            gate_up_ref.at[0, :, :, columns], wgu.at[:, :, columns], load_sem.at[k]
+        )
+
+    def load_d(n):
+        columns = pl.ds(n * nc, nc)
+        return pltpu.make_async_copy(
+            down_ref.at[0, :, columns], wd.at[:, columns], load_sem.at[nk + n]
+        )
+
+    for k in range(nk):
+        load_gu(k).start()
+    for n in range(nr):
+        load_d(n).start()
+
+    barrier = pltpu.get_barrier_semaphore()
+    for peer in [x_peer, y_peer, core_peer] + z_peers:
+        pl.semaphore_signal(barrier, inc=1, device_id=peer, device_id_type=MESH)
+    for k in range(nk):
+        xbuf[k, core, y, z, row] = tokens_ref[:, k * kc : (k + 1) * kc]
+    pl.semaphore_wait(barrier, 6)
+
+    def remote(src, dst, send, recv, peer):
+        return pltpu.make_async_remote_copy(
+            src_ref=src,
+            dst_ref=dst,
+            send_sem=send,
+            recv_sem=recv,
+            device_id=peer,
+            device_id_type=MESH,
+        )
+
+    def gather(k, index, part, peer):
+        return remote(part, part, g_send.at[k, index], g_recv.at[k, index], peer)
+
+    def gather_1(k):
+        part = xbuf.at[k, core, y, z, row]
+        return [gather(k, 0, part, x_peer if k % 2 == 0 else y_peer)]
+
+    def gather_2(k):
+        part = xbuf.at[k, core, y, z] if k % 2 == 0 else xbuf.at[k, core, :, z, row]
+        return [gather(k, 1 + i, part, z_peers[i]) for i in range(ZS - 1)]
+
+    def gather_3(k):
+        if k % 2 == 0:
+            return [gather(k, 4, xbuf.at[k, core, y], y_peer)]
+        return [gather(k, 4, xbuf.at[k, core, :, :, row], x_peer)]
+
+    def gather_4(k):
+        return [gather(k, 5, xbuf.at[k, core], core_peer)]
+
+    started = []
+
+    def start(copies):
+        for copy in copies:
+            copy.start()
+            started.append(copy)
+
+    def arrived(copies):
+        for copy in copies:
+            copy.wait_recv()
+
+    for k in range(nk):
+        start(gather_1(k))
+    for k in range(nk):
+        arrived(gather_1(k))
+        start(gather_2(k))
+    for k in range(nk):
+        arrived(gather_2(k))
+        start(gather_3(k))
+
+    member = ids_ref[...] == col
+    hit_row = jnp.sum(member.astype(jnp.float32), axis=0, keepdims=True)
+    weight_row = jnp.sum(jnp.where(member, weights_ref[...], 0.0), axis=0, keepdims=True)
+    place = lax.broadcasted_iota(jnp.int32, (tokens, tokens), 0)
+    other = lax.broadcasted_iota(jnp.int32, (tokens, tokens), 1)
+    group = tokens // ROWS
+    token = (
+        ((place // 4) % 2) * group
+        + ((place // 8) % 4) * 16
+        + ((place // 32) % 2) * 8
+        + (place // 64) * 4
+        + place % 4
+    )
+    earlier = (other < token) & (other // group == token // group)
+    rank = jnp.sum(jnp.where(earlier, hit_row, 0.0), axis=1, keepdims=True)
+    same = other == token
+    hit = jnp.sum(jnp.where(same, hit_row, 0.0), axis=1, keepdims=True)
+    weight = jnp.sum(jnp.where(same, weight_row, 0.0), axis=1, keepdims=True)
+    limit = capacity_ref[col].astype(jnp.float32)
+    combine = jnp.where((hit > 0.5) & (rank < limit), weight, 0.0)
+    combine = combine.astype(jnp.bfloat16).astype(jnp.float32)
+
+    def pass_on(k):
+        arrived(gather_3(k))
+        start(gather_4(k))
+
+    def send_hidden(h):
+        part = hid.at[row, h]
+        return [remote(part, part, h_send.at[h], h_recv.at[h], x_peer)]
+
+    def product(k, part, h):
+        return lax.dot_general(
+            x2d[k],
+            wgu[part, h * TILE : (h + 1) * TILE, k * kc : (k + 1) * kc],
+            (((1,), (1,)), ((), ())),
+            preferred_element_type=jnp.float32,
+        )
+
+    pass_on(0)
+    for k in range(nk):
+        if k + 1 < nk:
+            pass_on(k + 1)
+        arrived(gather_4(k))
+        block = xbuf[k].reshape(tokens // tok_dev, tok_dev, kc).astype(jnp.float32)
+        x2d[k] = block.reshape(tokens, kc).astype(jnp.bfloat16)
+        load_gu(k).wait()
+        for h in range(tiles):
+            gate = product(k, 0, h)
+            up = product(k, 1, h)
+            if k > 0:
+                gate = gate + acc[0, h]
+                up = up + acc[1, h]
+            if k < nk - 1:
+                acc[0, h] = gate
+                acc[1, h] = up
+            else:
+                hid[row, h] = (gate / (1.0 + jnp.exp(-gate)) * up).astype(jnp.bfloat16)
+                start(send_hidden(h))
+
+    def down_part(n, side):
+        total = None
+        for h in range(tiles):
+            rows = pl.ds(pl.multiple_of(side * hidden + h * TILE, TILE), TILE)
+            term = jnp.dot(
+                hid[side, h],
+                wd[rows, n * nc : (n + 1) * nc],
+                preferred_element_type=jnp.float32,
+            )
+            total = term if total is None else total + term
+        return total
+
+    def reduce_1(n):
+        return [remote(r1_out.at[n], r1_in.at[n], r_send.at[n, 0], r_recv.at[n, 0], core_peer)]
+
+    def reduce_2(n):
+        return [remote(r2_out.at[n], r2_in.at[n], r_send.at[n, 1], r_recv.at[n, 1], y_peer)]
+
+    def reduce_3(n):
+        return [
+            remote(
+                r3_out.at[n, z_places[i]],
+                r3_in.at[n, i],
+                r_send.at[n, 2 + i],
+                r_recv.at[n, 2 + i],
+                z_peers[i],
+            )
+            for i in range(ZS - 1)
+        ]
+
+    def reduce_4(n):
+        return [
+            remote(p3.at[n, 1 - row], r4_in.at[n], r_send.at[n, 5], r_recv.at[n, 5], x_peer)
+        ]
+
+    def after_core(n):
+        arrived(reduce_1(n))
+        both = zf[n, core] + r1_in[n].astype(jnp.float32)
+        p1[n] = both.reshape(p1.shape[1:])
+        r2_out[n] = p1[n, 1 - y].astype(jnp.bfloat16)
+        start(reduce_2(n))
+
+    def after_y(n):
+        arrived(reduce_2(n))
+        both = p1[n, y] + r2_in[n].astype(jnp.float32)
+        p2[n] = both.reshape(p2.shape[1:])
+        r3_out[n] = p2[n].astype(jnp.bfloat16)
+        start(reduce_3(n))
+
+    def after_z(n):
+        arrived(reduce_3(n))
+        total = p2[n, z]
+        for i in range(ZS - 1):
+            total = total + r3_in[n, i].astype(jnp.float32)
+        p3[n, 0] = total[:tok_dev].astype(jnp.bfloat16)
+        p3[n, 1] = total[tok_dev:].astype(jnp.bfloat16)
+        start(reduce_4(n))
+
+    for n in range(nr):
+        load_d(n).wait()
+        yacc[n] = down_part(n, row)
+    for h in range(tiles):
+        arrived(send_hidden(h))
+    for n in range(nr + 2):
+        if n < nr:
+            total = (yacc[n] + down_part(n, 1 - row)).astype(jnp.bfloat16)
+            scaled = total.astype(jnp.float32) * combine
+            zf[n] = scaled.reshape(zf.shape[1:])
+            r1_out[n] = zf[n, 1 - core].astype(jnp.bfloat16)
+            start(reduce_1(n))
+        if 1 <= n <= nr:
+            after_core(n - 1)
+        if n >= 2:
+            after_y(n - 2)
+    for n in range(nr):
+        after_z(n)
+    for n in range(nr):
+        mine = pl.ds(pl.multiple_of(row * half + n * nc, 128), nc)
+        theirs = pl.ds(pl.multiple_of((1 - row) * half + n * nc, 128), nc)
+        out_ref[:, mine] = p3[n, row]
+        arrived(reduce_4(n))
+        out_ref[:, theirs] = r4_in[n]
+    for copy in started:
+        copy.wait_send()
+
+
+def fused(tokens, gate_up, down, expert_ids, gate_weights, capacity):
+    nk, nr = 4, 4
+    tok_dev, width = tokens.shape
+    total = expert_ids.shape[0]
+    hidden = gate_up.shape[2]
+    half = down.shape[2]
+    kc, nc = width // nk, half // nr
+    tiles = hidden // TILE
+    vmem = pl.BlockSpec(memory_space=pltpu.VMEM)
+    hbm = pl.BlockSpec(memory_space=pl.ANY)
+    bf16, f32 = jnp.bfloat16, jnp.float32
+    per_core, per_y, per_z = total // CORES, total // (CORES * YS), total // (CORES * YS * ZS)
+    dma = pltpu.SemaphoreType.DMA
+    return pl.pallas_call(
+        functools.partial(fused_kernel, nk, nr),
+        out_shape=jax.ShapeDtypeStruct(tokens.shape, bf16),
+        in_specs=[vmem, vmem, vmem, pl.BlockSpec(memory_space=pltpu.SMEM), hbm, hbm],
+        out_specs=vmem,
+        scratch_shapes=[
+            pltpu.VMEM((2, hidden, width), bf16),
+            pltpu.VMEM((ROWS * hidden, half), bf16),
+            pltpu.VMEM((nk, CORES, YS, ZS, ROWS, tok_dev, kc), bf16),
+            pltpu.VMEM((nk, total, kc), bf16),
+            pltpu.VMEM((2, tiles, total, TILE), f32),
+            pltpu.VMEM((ROWS, tiles, total, TILE), bf16),
+            pltpu.VMEM((nr, total, nc), f32),
+            pltpu.VMEM((nr, CORES, per_core, nc), f32),
+            pltpu.VMEM((nr, per_core, nc), bf16),
+            pltpu.VMEM((nr, per_core, nc), bf16),
+            pltpu.VMEM((nr, YS, per_y, nc), f32),
+            pltpu.VMEM((nr, per_y, nc), bf16),
+            pltpu.VMEM((nr, per_y, nc), bf16),
+            pltpu.VMEM((nr, ZS, per_z, nc), f32),
+            pltpu.VMEM((nr, ZS, per_z, nc), bf16),
+            pltpu.VMEM((nr, ZS - 1, per_z, nc), bf16),
+            pltpu.VMEM((nr, ROWS, tok_dev, nc), bf16),
+            pltpu.VMEM((nr, tok_dev, nc), bf16),
+            dma((nk + nr,)),
+            dma((nk, 6)),
+            dma((nk, 6)),
+            dma((tiles,)),
+            dma((tiles,)),
+            dma((nr, 6)),
+            dma((nr, 6)),
+        ],
+        compiler_params=pltpu.CompilerParams(
+            collective_id=0, has_side_effects=True, vmem_limit_bytes=56 * 1024 * 1024
+        ),
+        cost_estimate=pl.CostEstimate(
+            flops=6 * total * hidden * width,
+            bytes_accessed=2 * (gate_up.size + down.size),
+            transcendentals=total * hidden,
+        ),
+    )(tokens, expert_ids.T, gate_weights.T, capacity, gate_up, down)
 
 
 def expert_slots(expert_ids, gate_weights, capacity, expert, block_rows, slot_cap):
@@ -86,4 +422,7 @@
         P(),
     )
     out_specs = P(("row", "col"), None)
-    return jax.shard_map(local, mesh=mesh, in_specs=in_specs, out_specs=out_specs, check_vma=False)
+    small = mesh.shape["row"] == ROWS and mesh.shape["col"] == CORES * YS * ZS
+    return jax.shard_map(
+        fused if small else local, mesh=mesh, in_specs=in_specs, out_specs=out_specs, check_vma=False
+    )

time: 165 us -> 53.8 us (0.33)
  waiting for transfers between devices: 81.8 us -> 0 us
  Pallas kernels: 0 us -> 52.1 us
  blocking collectives: 39 us -> 0 us
  matrix products: 24.2 us -> 0 us
  between operations: 13.5 us -> 0.01 us
  other arithmetic: 3.29 us -> 0 us
    reduce_scatter x1 -> x0, waiting for transfers between devices: 60.7 us -> none  [local(): lax.psum_scatter(jnp.dot(combine, outputs, preferred_element_type=jnp.flo...]
    pallas_call x0 -> x1, Pallas kernels: none -> 52.1 us  [fused(): pl.pallas_call(functools.partial(fused_kernel, nk, nr), out_shape=jax.Sha...]
    all_gather x2 -> x0, blocking collectives: 32.4 us -> none  [the longest x1 26.1 us: local(): group_tokens = lax.all_gather(tokens, 'col', axis=0, tiled=True)]
    dot_general x4 -> x0, matrix products: 24.2 us -> none  [the longest x1 7.85 us: local(): lax.dot_general(piece, w_gate, contract, preferred_element_type=jnp.float32)]
    all_gather x1 -> x0, waiting for transfers between devices: 21.1 us -> none  [local(): piece = lax.all_gather(picked, 'row', axis=0, tiled=True)]
    all_to_all x1 -> x0, blocking collectives: 6.6 us -> none  [local(): lax.all_to_all(summed.astype(jnp.bfloat16), 'row', split_axis=0, concat_a...]
  transfers between devices with their start and end apart: 2 -> 0, of which waited for: 2 -> 0; matrix products, arithmetic and copies ran while one was open for 1% -> 0% of each run, Pallas kernels for 0% -> 0%
where the time goes in v1:
time: 53.8 us; the launch traced here: 53.6 us
  Pallas kernels  52.1 us (97%)
  local copies, waits for them, and re-layouts  1.46 us (3%)
    pallas_call x1, Pallas kernels, fused(): pl.pallas_call(functools.partial(fused_kernel, nk, nr), out_shape=jax.Sha...  52.1 us
    unnamed x1, local copies, waits for them, and re-layouts  1.46 us

profile of v1, /device:TPU:0, one launch (start us, length us, event | category | flops | bytes accessed | tf_op | source)
XLA Modules:
  0.0 53.6 jit_solution(4303210474651034615)
XLA Ops:
  0.0 52.1 %shard_map.64 = bf16[4,7168]{1,0:T(4,128)(2,1)} custom-call(bf16[4,7168]{1,0:T(4,128)(2,1)} %tokens_ref.1, s32[8,128]{1,0:T(8,128)} %bitcast.2, f32[8,128]{1,0:T(8,128)} %bitcast.3, s32[16]{0:T(128)} %capacity_ref.1, bf16[1,2,768,7168]{3,2,1,0:T(8,128)(2,1)} %gate_up_ref.1, bf16[1,1536,3584]{2,1,0:T(8,128)(2,1)} %down_ref.1), custom_call_target="tpu_custom_call" | custom-call | flops 4227858432 | bytes 33030144 | tf_op jit(solution)/shard_map/pallas_call | solution.py:302
  52.1 1.5 %copy.8 = bf16[4,7168]{1,0:T(4,128)(2,1)} copy(bf16[4,7168]{1,0:T(4,128)(2,1)} %shard_map.64) | data formatting | bytes 114688

commit v2 on v1

--- a/solution.py
+++ b/solution.py
@@ -171,10 +171,10 @@
         part = hid.at[row, h]
         return [remote(part, part, h_send.at[h], h_recv.at[h], x_peer)]
 
-    def product(k, part, h):
+    def product(k, part, first, count):
         return lax.dot_general(
+            wgu[part, first : first + count, k * kc : (k + 1) * kc],
             x2d[k],
-            wgu[part, h * TILE : (h + 1) * TILE, k * kc : (k + 1) * kc],
             (((1,), (1,)), ((), ())),
             preferred_element_type=jnp.float32,
         )
@@ -187,18 +187,18 @@
         block = xbuf[k].reshape(tokens // tok_dev, tok_dev, kc).astype(jnp.float32)
         x2d[k] = block.reshape(tokens, kc).astype(jnp.bfloat16)
         load_gu(k).wait()
+        if k < nk - 1:
+            for part in range(2):
+                term = product(k, part, 0, hidden)
+                acc[part] = term if k == 0 else acc[part] + term
+            continue
         for h in range(tiles):
-            gate = product(k, 0, h)
-            up = product(k, 1, h)
-            if k > 0:
-                gate = gate + acc[0, h]
-                up = up + acc[1, h]
-            if k < nk - 1:
-                acc[0, h] = gate
-                acc[1, h] = up
-            else:
-                hid[row, h] = (gate / (1.0 + jnp.exp(-gate)) * up).astype(jnp.bfloat16)
-                start(send_hidden(h))
+            rows = slice(h * TILE, (h + 1) * TILE)
+            gate = acc[0, rows] + product(k, 0, h * TILE, TILE)
+            up = acc[1, rows] + product(k, 1, h * TILE, TILE)
+            act = gate / (1.0 + jnp.exp(-gate)) * up
+            hid[row, h] = act.T.astype(jnp.bfloat16)
+            start(send_hidden(h))
 
     def down_part(n, side):
         total = None
@@ -309,7 +309,7 @@
             pltpu.VMEM((ROWS * hidden, half), bf16),
             pltpu.VMEM((nk, CORES, YS, ZS, ROWS, tok_dev, kc), bf16),
             pltpu.VMEM((nk, total, kc), bf16),
-            pltpu.VMEM((2, tiles, total, TILE), f32),
+            pltpu.VMEM((2, hidden, total), f32),
             pltpu.VMEM((ROWS, tiles, total, TILE), bf16),
             pltpu.VMEM((nr, total, nc), f32),
             pltpu.VMEM((nr, CORES, per_core, nc), f32),

time: 53.8 us -> 53.1 us (0.987)
  Pallas kernels: 52.1 us -> 51.5 us
    pallas_call x1, Pallas kernels: 52.1 us -> 51.5 us  [fused(): pl.pallas_call(functools.partial(fused_kernel, nk, nr), out_shape=jax.Sha...]
where the time goes in v2:
time: 53.1 us; the launch traced here: 52.9 us
  Pallas kernels  51.5 us (97%)
  local copies, waits for them, and re-layouts  1.46 us (3%)
    pallas_call x1, Pallas kernels, fused(): pl.pallas_call(functools.partial(fused_kernel, nk, nr), out_shape=jax.Sha...  51.5 us
    unnamed x1, local copies, waits for them, and re-layouts  1.46 us

profile of v2, /device:TPU:0, one launch (start us, length us, event | category | flops | bytes accessed | tf_op | source)
XLA Modules:
  0.0 52.9 jit_solution(12850326622269760088)
XLA Ops:
  0.0 51.5 %shard_map.64 = bf16[4,7168]{1,0:T(4,128)(2,1)} custom-call(bf16[4,7168]{1,0:T(4,128)(2,1)} %tokens_ref.1, s32[8,128]{1,0:T(8,128)} %bitcast.2, f32[8,128]{1,0:T(8,128)} %bitcast.3, s32[16]{0:T(128)} %capacity_ref.1, bf16[1,2,768,7168]{3,2,1,0:T(8,128)(2,1)} %gate_up_ref.1, bf16[1,1536,3584]{2,1,0:T(8,128)(2,1)} %down_ref.1), custom_call_target="tpu_custom_call" | custom-call | flops 4227858432 | bytes 33030144 | tf_op jit(solution)/shard_map/pallas_call | solution.py:302
  51.5 1.5 %copy.8 = bf16[4,7168]{1,0:T(4,128)(2,1)} copy(bf16[4,7168]{1,0:T(4,128)(2,1)} %shard_map.64) | data formatting | bytes 114688

commit v3 on v2

--- a/solution.py
+++ b/solution.py
@@ -10,6 +10,7 @@
 TOP = 8
 MESH = pl.DeviceIdType.MESH
 CORES, YS, ZS, ROWS = 2, 2, 4, 2
+ORDERS = ("xzyc", "zxyc", "yzxc", "zyxc")
 TILE = 256
 
 
@@ -102,24 +103,23 @@
             device_id_type=MESH,
         )
 
-    def gather(k, index, part, peer):
-        return remote(part, part, g_send.at[k, index], g_recv.at[k, index], peer)
-
-    def gather_1(k):
-        part = xbuf.at[k, core, y, z, row]
-        return [gather(k, 0, part, x_peer if k % 2 == 0 else y_peer)]
-
-    def gather_2(k):
-        part = xbuf.at[k, core, y, z] if k % 2 == 0 else xbuf.at[k, core, :, z, row]
-        return [gather(k, 1 + i, part, z_peers[i]) for i in range(ZS - 1)]
-
-    def gather_3(k):
-        if k % 2 == 0:
-            return [gather(k, 4, xbuf.at[k, core, y], y_peer)]
-        return [gather(k, 4, xbuf.at[k, core, :, :, row], x_peer)]
-
-    def gather_4(k):
-        return [gather(k, 5, xbuf.at[k, core], core_peer)]
+    peers = {"x": [x_peer], "z": z_peers, "y": [y_peer], "c": [core_peer]}
+    first_sem = {"x": 0, "z": 1, "y": 4, "c": 5}
+
+    def gather(k, stage):
+        order = ORDERS[k % len(ORDERS)]
+        done, axis = order[:stage], order[stage]
+        part = xbuf.at[
+            k,
+            core,
+            slice(None) if "y" in done else y,
+            slice(None) if "z" in done else z,
+            slice(None) if "x" in done else row,
+        ]
+        return [
+            remote(part, part, g_send.at[k, first_sem[axis] + i], g_recv.at[k, first_sem[axis] + i], peer)
+            for i, peer in enumerate(peers[axis])
+        ]
 
     started = []
 
@@ -132,14 +132,14 @@
         for copy in copies:
             copy.wait_recv()
 
+    def pass_on(k, stage):
+        arrived(gather(k, stage - 1))
+        start(gather(k, stage))
+
     for k in range(nk):
-        start(gather_1(k))
+        start(gather(k, 0))
     for k in range(nk):
-        arrived(gather_1(k))
-        start(gather_2(k))
-    for k in range(nk):
-        arrived(gather_2(k))
-        start(gather_3(k))
+        pass_on(k, 1)
 
     member = ids_ref[...] == col
     hit_row = jnp.sum(member.astype(jnp.float32), axis=0, keepdims=True)
@@ -163,10 +163,6 @@
     combine = jnp.where((hit > 0.5) & (rank < limit), weight, 0.0)
     combine = combine.astype(jnp.bfloat16).astype(jnp.float32)
 
-    def pass_on(k):
-        arrived(gather_3(k))
-        start(gather_4(k))
-
     def send_hidden(h):
         part = hid.at[row, h]
         return [remote(part, part, h_send.at[h], h_recv.at[h], x_peer)]
@@ -179,11 +175,15 @@
             preferred_element_type=jnp.float32,
         )
 
-    pass_on(0)
-    for k in range(nk):
-        if k + 1 < nk:
-            pass_on(k + 1)
-        arrived(gather_4(k))
+    for step in range(nk + 2):
+        if step < nk:
+            pass_on(step, 2)
+        if 1 <= step <= nk:
+            pass_on(step - 1, 3)
+        if step < 2:
+            continue
+        k = step - 2
+        arrived(gather(k, 3))
         block = xbuf[k].reshape(tokens // tok_dev, tok_dev, kc).astype(jnp.float32)
         x2d[k] = block.reshape(tokens, kc).astype(jnp.bfloat16)
         load_gu(k).wait()
@@ -263,7 +263,7 @@
         yacc[n] = down_part(n, row)
     for h in range(tiles):
         arrived(send_hidden(h))
-    for n in range(nr + 2):
+    for n in range(nr + 3):
         if n < nr:
             total = (yacc[n] + down_part(n, 1 - row)).astype(jnp.bfloat16)
             scaled = total.astype(jnp.float32) * combine
@@ -272,10 +272,10 @@
             start(reduce_1(n))
         if 1 <= n <= nr:
             after_core(n - 1)
-        if n >= 2:
+        if 2 <= n <= nr + 1:
             after_y(n - 2)
-    for n in range(nr):
-        after_z(n)
+        if n >= 3:
+            after_z(n - 3)
     for n in range(nr):
         mine = pl.ds(pl.multiple_of(row * half + n * nc, 128), nc)
         theirs = pl.ds(pl.multiple_of((1 - row) * half + n * nc, 128), nc)

time: 53.1 us -> 55.5 us (1.045)
  Pallas kernels: 51.5 us -> 53.8 us
    pallas_call x1, Pallas kernels: 51.5 us -> 53.8 us  [fused(): pl.pallas_call(functools.partial(fused_kernel, nk, nr), out_shape=jax.Sha...]
where the time goes in v3:
time: 55.5 us; the launch traced here: 55.3 us
  Pallas kernels  53.8 us (97%)
  local copies, waits for them, and re-layouts  1.46 us (3%)
    pallas_call x1, Pallas kernels, fused(): pl.pallas_call(functools.partial(fused_kernel, nk, nr), out_shape=jax.Sha...  53.8 us
    unnamed x1, local copies, waits for them, and re-layouts  1.46 us

profile of v3, /device:TPU:0, one launch (start us, length us, event | category | flops | bytes accessed | tf_op | source)
XLA Modules:
  0.0 55.3 jit_solution(1448115153464026186)
XLA Ops:
  0.0 53.8 %shard_map.64 = bf16[4,7168]{1,0:T(4,128)(2,1)} custom-call(bf16[4,7168]{1,0:T(4,128)(2,1)} %tokens_ref.1, s32[8,128]{1,0:T(8,128)} %bitcast.2, f32[8,128]{1,0:T(8,128)} %bitcast.3, s32[16]{0:T(128)} %capacity_ref.1, bf16[1,2,768,7168]{3,2,1,0:T(8,128)(2,1)} %gate_up_ref.1, bf16[1,1536,3584]{2,1,0:T(8,128)(2,1)} %down_ref.1), custom_call_target="tpu_custom_call" | custom-call | flops 4227858432 | bytes 33030144 | tf_op jit(solution)/shard_map/pallas_call | solution.py:302
  53.8 1.5 %copy.8 = bf16[4,7168]{1,0:T(4,128)(2,1)} copy(bf16[4,7168]{1,0:T(4,128)(2,1)} %shard_map.64) | data formatting | bytes 114688

commit v4 on v3

--- a/solution.py
+++ b/solution.py
@@ -81,10 +81,27 @@
             down_ref.at[0, :, columns], wd.at[:, columns], load_sem.at[nk + n]
         )
 
-    for k in range(nk):
-        load_gu(k).start()
-    for n in range(nr):
-        load_d(n).start()
+    def start_gu(k):
+        columns = pl.ds(k * kc, kc)
+        for part in range(2):
+            for h in range(tiles):
+                rows = pl.ds(h * TILE, TILE)
+                pltpu.make_async_copy(
+                    gate_up_ref.at[0, part, rows, columns],
+                    wgu.at[part, rows, columns],
+                    load_sem.at[k],
+                ).start(priority=1)
+
+    def start_d(n):
+        columns = pl.ds(n * nc, nc)
+        for h in range(ROWS * tiles):
+            rows = pl.ds(h * TILE, TILE)
+            pltpu.make_async_copy(
+                down_ref.at[0, rows, columns], wd.at[rows, columns], load_sem.at[nk + n]
+            ).start(priority=1)
+
+    start_gu(0)
+    start_gu(1)
 
     barrier = pltpu.get_barrier_semaphore()
     for peer in [x_peer, y_peer, core_peer] + z_peers:
@@ -140,6 +157,7 @@
         start(gather(k, 0))
     for k in range(nk):
         pass_on(k, 1)
+    start_gu(2)
 
     member = ids_ref[...] == col
     hit_row = jnp.sum(member.astype(jnp.float32), axis=0, keepdims=True)
@@ -178,6 +196,12 @@
     for step in range(nk + 2):
         if step < nk:
             pass_on(step, 2)
+        if step == 1:
+            for k in range(3, nk):
+                start_gu(k)
+        if 2 <= step < 4:
+            for n in range(step - 2, nr, 2):
+                start_d(n)
         if 1 <= step <= nk:
             pass_on(step - 1, 3)
         if step < 2:

time: 55.5 us -> 55.5 us (level)
  no operation moved by 1% of the time
where the time goes in v4:
time: 55.5 us; the launch traced here: 55.3 us
  Pallas kernels  53.9 us (97%)
  local copies, waits for them, and re-layouts  1.46 us (3%)
    pallas_call x1, Pallas kernels, fused(): pl.pallas_call(functools.partial(fused_kernel, nk, nr), out_shape=jax.Sha...  53.9 us
    unnamed x1, local copies, waits for them, and re-layouts  1.46 us

profile of v4, /device:TPU:0, one launch (start us, length us, event | category | flops | bytes accessed | tf_op | source)
XLA Modules:
  0.0 55.3 jit_solution(9851419334892922742)
XLA Ops:
  0.0 53.9 %shard_map.64 = bf16[4,7168]{1,0:T(4,128)(2,1)} custom-call(bf16[4,7168]{1,0:T(4,128)(2,1)} %tokens_ref.1, s32[8,128]{1,0:T(8,128)} %bitcast.2, f32[8,128]{1,0:T(8,128)} %bitcast.3, s32[16]{0:T(128)} %capacity_ref.1, bf16[1,2,768,7168]{3,2,1,0:T(8,128)(2,1)} %gate_up_ref.1, bf16[1,1536,3584]{2,1,0:T(8,128)(2,1)} %down_ref.1), custom_call_target="tpu_custom_call" | custom-call | flops 4227858432 | bytes 33030144 | tf_op jit(solution)/shard_map/pallas_call | solution.py:326
  53.9 1.5 %copy.8 = bf16[4,7168]{1,0:T(4,128)(2,1)} copy(bf16[4,7168]{1,0:T(4,128)(2,1)} %shard_map.64) | data formatting | bytes 114688

commit v5 on v3

--- a/solution.py
+++ b/solution.py
@@ -10,7 +10,7 @@
 TOP = 8
 MESH = pl.DeviceIdType.MESH
 CORES, YS, ZS, ROWS = 2, 2, 4, 2
-ORDERS = ("xzyc", "zxyc", "yzxc", "zyxc")
+ORDERS = ("xzyc", "yzxc")
 TILE = 256
 
 
@@ -287,7 +287,7 @@
 
 
 def fused(tokens, gate_up, down, expert_ids, gate_weights, capacity):
-    nk, nr = 4, 4
+    nk, nr = 7, 7
     tok_dev, width = tokens.shape
     total = expert_ids.shape[0]
     hidden = gate_up.shape[2]

time: 55.5 us -> 65.7 us (1.18)
  Pallas kernels: 53.8 us -> 64 us
    pallas_call x1, Pallas kernels: 53.8 us -> 64 us  [fused(): pl.pallas_call(functools.partial(fused_kernel, nk, nr), out_shape=jax.Sha...]
where the time goes in v5:
time: 65.7 us; the launch traced here: 65.5 us
  Pallas kernels  64 us (97%)
  local copies, waits for them, and re-layouts  1.46 us (2%)
    pallas_call x1, Pallas kernels, fused(): pl.pallas_call(functools.partial(fused_kernel, nk, nr), out_shape=jax.Sha...  64 us
    unnamed x1, local copies, waits for them, and re-layouts  1.46 us

profile of v5, /device:TPU:0, one launch (start us, length us, event | category | flops | bytes accessed | tf_op | source)
XLA Modules:
  0.0 65.5 jit_solution(7361380744808640111)
XLA Ops:
  0.0 64.0 %shard_map.64 = bf16[4,7168]{1,0:T(4,128)(2,1)} custom-call(bf16[4,7168]{1,0:T(4,128)(2,1)} %tokens_ref.1, s32[8,128]{1,0:T(8,128)} %bitcast.2, f32[8,128]{1,0:T(8,128)} %bitcast.3, s32[16]{0:T(128)} %capacity_ref.1, bf16[1,2,768,7168]{3,2,1,0:T(8,128)(2,1)} %gate_up_ref.1, bf16[1,1536,3584]{2,1,0:T(8,128)(2,1)} %down_ref.1), custom_call_target="tpu_custom_call" | custom-call | flops 4227858432 | bytes 33030144 | tf_op jit(solution)/shard_map/pallas_call | solution.py:302
  64.0 1.5 %copy.8 = bf16[4,7168]{1,0:T(4,128)(2,1)} copy(bf16[4,7168]{1,0:T(4,128)(2,1)} %shard_map.64) | data formatting | bytes 114688

commit v6 on v5

--- a/solution.py
+++ b/solution.py
@@ -287,7 +287,7 @@
 
 
 def fused(tokens, gate_up, down, expert_ids, gate_weights, capacity):
-    nk, nr = 7, 7
+    nk, nr = 2, 2
     tok_dev, width = tokens.shape
     total = expert_ids.shape[0]
     hidden = gate_up.shape[2]

time: 65.7 us -> 54.3 us (0.83)
  Pallas kernels: 64 us -> 52.7 us
    pallas_call x1, Pallas kernels: 64 us -> 52.7 us  [fused(): pl.pallas_call(functools.partial(fused_kernel, nk, nr), out_shape=jax.Sha...]
where the time goes in v6:
time: 54.3 us; the launch traced here: 54.1 us
  Pallas kernels  52.7 us (97%)
  local copies, waits for them, and re-layouts  1.46 us (3%)
    pallas_call x1, Pallas kernels, fused(): pl.pallas_call(functools.partial(fused_kernel, nk, nr), out_shape=jax.Sha...  52.7 us
    unnamed x1, local copies, waits for them, and re-layouts  1.46 us

profile of v6, /device:TPU:0, one launch (start us, length us, event | category | flops | bytes accessed | tf_op | source)
XLA Modules:
  0.0 54.1 jit_solution(14828386448765545149)
XLA Ops:
  0.0 52.7 %shard_map.64 = bf16[4,7168]{1,0:T(4,128)(2,1)} custom-call(bf16[4,7168]{1,0:T(4,128)(2,1)} %tokens_ref.1, s32[8,128]{1,0:T(8,128)} %bitcast.2, f32[8,128]{1,0:T(8,128)} %bitcast.3, s32[16]{0:T(128)} %capacity_ref.1, bf16[1,2,768,7168]{3,2,1,0:T(8,128)(2,1)} %gate_up_ref.1, bf16[1,1536,3584]{2,1,0:T(8,128)(2,1)} %down_ref.1), custom_call_target="tpu_custom_call" | custom-call | flops 4227858432 | bytes 33030144 | tf_op jit(solution)/shard_map/pallas_call | solution.py:302
  52.7 1.5 %copy.8 = bf16[4,7168]{1,0:T(4,128)(2,1)} copy(bf16[4,7168]{1,0:T(4,128)(2,1)} %shard_map.64) | data formatting | bytes 114688

commit v7 on v6

--- a/solution.py
+++ b/solution.py
@@ -175,14 +175,15 @@
             preferred_element_type=jnp.float32,
         )
 
-    for step in range(nk + 2):
-        if step < nk:
-            pass_on(step, 2)
-        if 1 <= step <= nk:
-            pass_on(step - 1, 3)
-        if step < 2:
-            continue
-        k = step - 2
+    for k in range(nk):
+        pass_on(k, 2)
+        if k >= 2:
+            pass_on(k - 2, 3)
+    for k in range(nk):
+        if k == 0:
+            pass_on(nk - 2, 3)
+        if k == 1:
+            pass_on(nk - 1, 3)
         arrived(gather(k, 3))
         block = xbuf[k].reshape(tokens // tok_dev, tok_dev, kc).astype(jnp.float32)
         x2d[k] = block.reshape(tokens, kc).astype(jnp.bfloat16)
@@ -263,19 +264,20 @@
         yacc[n] = down_part(n, row)
     for h in range(tiles):
         arrived(send_hidden(h))
-    for n in range(nr + 3):
-        if n < nr:
-            total = (yacc[n] + down_part(n, 1 - row)).astype(jnp.bfloat16)
-            scaled = total.astype(jnp.float32) * combine
-            zf[n] = scaled.reshape(zf.shape[1:])
-            r1_out[n] = zf[n, 1 - core].astype(jnp.bfloat16)
-            start(reduce_1(n))
-        if 1 <= n <= nr:
-            after_core(n - 1)
-        if 2 <= n <= nr + 1:
-            after_y(n - 2)
-        if n >= 3:
-            after_z(n - 3)
+    for n in range(nr):
+        total = (yacc[n] + down_part(n, 1 - row)).astype(jnp.bfloat16)
+        scaled = total.astype(jnp.float32) * combine
+        zf[n] = scaled.reshape(zf.shape[1:])
+        r1_out[n] = zf[n, 1 - core].astype(jnp.bfloat16)
+        start(reduce_1(n))
+        if n >= 2:
+            after_core(n - 2)
+    for n in range(nr - 2, nr):
+        after_core(n)
+    for n in range(nr):
+        after_y(n)
+    for n in range(nr):
+        after_z(n)
     for n in range(nr):
         mine = pl.ds(pl.multiple_of(row * half + n * nc, 128), nc)
         theirs = pl.ds(pl.multiple_of((1 - row) * half + n * nc, 128), nc)
@@ -287,7 +289,7 @@
 
 
 def fused(tokens, gate_up, down, expert_ids, gate_weights, capacity):
-    nk, nr = 2, 2
+    nk, nr = 4, 4
     tok_dev, width = tokens.shape
     total = expert_ids.shape[0]
     hidden = gate_up.shape[2]

time: 54.3 us -> 51.6 us (0.950)
  Pallas kernels: 52.7 us -> 49.9 us
    pallas_call x1, Pallas kernels: 52.7 us -> 49.9 us  [fused(): pl.pallas_call(functools.partial(fused_kernel, nk, nr), out_shape=jax.Sha...]
where the time goes in v7:
time: 51.6 us; the launch traced here: 51.4 us
  Pallas kernels  49.9 us (97%)
  local copies, waits for them, and re-layouts  1.46 us (3%)
    pallas_call x1, Pallas kernels, fused(): pl.pallas_call(functools.partial(fused_kernel, nk, nr), out_shape=jax.Sha...  49.9 us
    unnamed x1, local copies, waits for them, and re-layouts  1.46 us

profile of v7, /device:TPU:0, one launch (start us, length us, event | category | flops | bytes accessed | tf_op | source)
XLA Modules:
  0.0 51.4 jit_solution(17419795643447882935)
XLA Ops:
  0.0 49.9 %shard_map.64 = bf16[4,7168]{1,0:T(4,128)(2,1)} custom-call(bf16[4,7168]{1,0:T(4,128)(2,1)} %tokens_ref.1, s32[8,128]{1,0:T(8,128)} %bitcast.2, f32[8,128]{1,0:T(8,128)} %bitcast.3, s32[16]{0:T(128)} %capacity_ref.1, bf16[1,2,768,7168]{3,2,1,0:T(8,128)(2,1)} %gate_up_ref.1, bf16[1,1536,3584]{2,1,0:T(8,128)(2,1)} %down_ref.1), custom_call_target="tpu_custom_call" | custom-call | flops 4227858432 | bytes 33030144 | tf_op jit(solution)/shard_map/pallas_call | solution.py:304
  49.9 1.5 %copy.8 = bf16[4,7168]{1,0:T(4,128)(2,1)} copy(bf16[4,7168]{1,0:T(4,128)(2,1)} %shard_map.64) | data formatting | bytes 114688

commit v8 on v7

--- a/solution.py
+++ b/solution.py
@@ -10,7 +10,7 @@
 TOP = 8
 MESH = pl.DeviceIdType.MESH
 CORES, YS, ZS, ROWS = 2, 2, 4, 2
-ORDERS = ("xzyc", "yzxc")
+ORDERS = ("xzyc", "yzxc", "zxyc", "zyxc")
 TILE = 256
 
 

time: 51.6 us -> 50.4 us (0.977)
  Pallas kernels: 49.9 us -> 48.7 us
    pallas_call x1, Pallas kernels: 49.9 us -> 48.7 us  [fused(): pl.pallas_call(functools.partial(fused_kernel, nk, nr), out_shape=jax.Sha...]
where the time goes in v8:
time: 50.4 us; the launch traced here: 50.2 us
  Pallas kernels  48.7 us (97%)
  local copies, waits for them, and re-layouts  1.46 us (3%)
    pallas_call x1, Pallas kernels, fused(): pl.pallas_call(functools.partial(fused_kernel, nk, nr), out_shape=jax.Sha...  48.7 us
    unnamed x1, local copies, waits for them, and re-layouts  1.46 us

profile of v8, /device:TPU:0, one launch (start us, length us, event | category | flops | bytes accessed | tf_op | source)
XLA Modules:
  0.0 50.2 jit_solution(5005257227256904136)
XLA Ops:
  0.0 48.7 %shard_map.64 = bf16[4,7168]{1,0:T(4,128)(2,1)} custom-call(bf16[4,7168]{1,0:T(4,128)(2,1)} %tokens_ref.1, s32[8,128]{1,0:T(8,128)} %bitcast.2, f32[8,128]{1,0:T(8,128)} %bitcast.3, s32[16]{0:T(128)} %capacity_ref.1, bf16[1,2,768,7168]{3,2,1,0:T(8,128)(2,1)} %gate_up_ref.1, bf16[1,1536,3584]{2,1,0:T(8,128)(2,1)} %down_ref.1), custom_call_target="tpu_custom_call" | custom-call | flops 4227858432 | bytes 33030144 | tf_op jit(solution)/shard_map/pallas_call | solution.py:304
  48.7 1.5 %copy.8 = bf16[4,7168]{1,0:T(4,128)(2,1)} copy(bf16[4,7168]{1,0:T(4,128)(2,1)} %shard_map.64) | data formatting | bytes 114688
